TPU v7x, 128 devices: a whole 4x4x4 slice. The times are simulated.
128 devices in a mesh: agent: 8 (over z, core), cluster: 16 (over x, y).
Axes of the slice: x: 4, y: 4, z: 4, core: 2. Of those that a mesh axis runs over, the one named last changes fastest.
Arguments:
- jacobians: bfloat16 [72, 65536], P(None, ('agent', 'cluster')), may hold values from -6 to 6
- point_hessians: float32 [6, 65536], P(None, ('agent', 'cluster')), as said below
- cameras: int32 [4, 65536], P(None, ('agent', 'cluster')), may hold values from 0 to 255, as said below
- tiles: int32 [65536], P(('agent', 'cluster')), may hold values from 0 to 127, as said below
- damping: int32 [8], replicated, may hold values from 1 to 16
Outputs:
- band: float32 [12288, 24576], P('agent', 'cluster')
Inputs may be any that keep to these rules, and one draw needn't show every extreme that they name: `point_hessians`: the point block of every track is symmetric positive definite; each off-diagonal entry is at most 0.45 times the square root of the product of its two diagonal entries, and the diagonal entries are positive. The 4 cameras of one track are distinct. `tiles`: among the 512 tracks of one device (aligned blocks of the array) at most 12 feed one tile; one tile is fed by exactly 12 tracks of every device.
All inputs are finite; a program needn't handle non-finite values.
Results may differ from a plain program's by a relative error of at most 0.00086.
Values may be sent and summed in bfloat16 or wider, within the bound.
A program may use at most 256 MiB of HBM per device.

v0:
```python
import jax
import jax.numpy as jnp
from jax import lax
from jax.sharding import PartitionSpec as P

CAMS = 256


def spread(shard, axis, root):
    mine = lax.axis_index(axis) == root
    return lax.psum(jnp.where(mine, shard, jnp.zeros_like(shard)), axis)


def point_inverse(hess):
    a, b, c, d, e, f = (hess[0], hess[1], hess[2], hess[3], hess[4], hess[5])
    c00 = b * c - f * f
    c11 = a * c - e * e
    c22 = a * b - d * d
    c01 = e * f - d * c
    c02 = d * f - e * b
    c12 = d * e - a * f
    det = a * c00 + d * c01 + e * c02
    rows = jnp.stack(
        [jnp.stack([c00, c01, c02]), jnp.stack([c01, c11, c12]), jnp.stack([c02, c12, c22])]
    )
    return rows / det


def assemble(weighted, plain, cams, diag_flag):
    obs_count = cams.shape[0]
    total = cams.shape[1]
    order = 6 * CAMS
    block = 512
    obs_idx = jnp.arange(obs_count, dtype=jnp.int32)
    left_w = jnp.logical_or(diag_flag, obs_idx < 2).astype(jnp.bfloat16)
    right_w = jnp.logical_or(diag_flag, obs_idx >= 2).astype(jnp.bfloat16)
    tile = jnp.zeros((order, order), jnp.float32)
    for start in range(0, total, block):
        cam_blk = cams[:, start : start + block]
        hot = (cam_blk[:, None, :] == jnp.arange(CAMS, dtype=jnp.int32)[None, :, None]).astype(
            jnp.bfloat16
        )
        wgt_blk = weighted[:, start : start + block].reshape(obs_count, 6, 3, block)
        jac_blk = plain[:, start : start + block].reshape(obs_count, 6, 3, block)
        left = jnp.einsum(
            "oks,oris->kris",
            hot * left_w[:, None, None],
            wgt_blk,
            preferred_element_type=jnp.float32,
        )
        right = jnp.einsum(
            "oks,oris->kris",
            hot * right_w[:, None, None],
            jac_blk,
            preferred_element_type=jnp.float32,
        )
        left = left.astype(jnp.bfloat16).reshape(order, 3 * block)
        right = right.astype(jnp.bfloat16).reshape(order, 3 * block)
        tile = tile + lax.dot_general(
            left, right, (((1,), (1,)), ((), ())), preferred_element_type=jnp.float32
        )
    return tile


def per_device(jacobians, point_hessians, cameras, tiles, damping):
    agents = lax.axis_size("agent")
    clusters = lax.axis_size("cluster")
    devices = agents * clusters
    local = tiles.shape[0]
    obs_count = cameras.shape[0]
    room = 3 * local // devices
    width = devices * room
    pinv = point_inverse(point_hessians)
    jac = jacobians.astype(jnp.float32).reshape(obs_count, 6, 3, local)
    weighted = jnp.einsum("oris,ijs->orjs", jac, pinv, precision=lax.Precision.HIGHEST)
    weighted = weighted.astype(jnp.bfloat16).reshape(18 * obs_count, local)
    onehot = (tiles[:, None] == jnp.arange(devices, dtype=jnp.int32)[None, :]).astype(jnp.int32)
    rank = jnp.sum(jnp.cumsum(onehot, axis=0) * onehot, axis=1) - 1
    slot = tiles * room + rank
    wgt_buf = jnp.zeros((18 * obs_count, width), jnp.bfloat16).at[:, slot].set(weighted)
    jac_buf = jnp.zeros((18 * obs_count, width), jnp.bfloat16).at[:, slot].set(jacobians)
    cam_buf = jnp.zeros((obs_count, width), jnp.int32).at[:, slot].set(cameras)
    wgt_in, jac_in, cam_in = (
        lax.all_to_all(wgt_buf, ("agent", "cluster"), split_axis=1, concat_axis=1, tiled=True),
        lax.all_to_all(jac_buf, ("agent", "cluster"), split_axis=1, concat_axis=1, tiled=True),
        lax.all_to_all(cam_buf, ("agent", "cluster"), split_axis=1, concat_axis=1, tiled=True),
    )
    row = lax.axis_index("agent")
    col = lax.axis_index("cluster")
    on_diag = row == col
    tile = assemble(wgt_in, jac_in, cam_in, on_diag)
    order = tile.shape[0]
    scale = (
        jnp.sum(jnp.where(jnp.arange(damping.shape[0], dtype=jnp.int32) == row, damping, 0)).astype(
            jnp.float32
        )
        / 8.0
    )

    def damped_factor(own):
        return jnp.linalg.cholesky(own + scale * jnp.diag(jnp.diagonal(own) + 1.0))

    empty = jnp.zeros((order, order), jnp.float32)
    lower = lax.cond(on_diag, lambda: damped_factor(tile), lambda: empty)
    lower = spread(lower, "cluster", row)
    result = lax.cond(
        on_diag, lambda: lower, lambda: jax.scipy.linalg.solve_triangular(lower, tile, lower=True)
    )
    return result


def solution(mesh):
    in_specs = (
        P(None, ("agent", "cluster")),
        P(None, ("agent", "cluster")),
        P(None, ("agent", "cluster")),
        P(("agent", "cluster")),
        P(),
    )
    out_specs = P("agent", "cluster")
    return jax.shard_map(
        per_device, mesh=mesh, in_specs=in_specs, out_specs=out_specs, check_vma=False
    )
```

profile of v0, /device:TPU:115, one launch (start us, length us, event | category | flops | bytes accessed | tf_op | source)
XLA Modules:
  0.0 1080.6 jit_solution(13977651274040426218)
XLA Ops:
  13.5 10.1 all-to-all-start.1
  28.2 2.9 copy.121
  31.1 5.3 convert_bitcast_fusion.6
  37.1 2.5 scatter_custom_fusion.2
  46.6 9.8 all-to-all-start.2
  57.0 4.6 all-to-all-done.2
  61.6 10.2 all-to-all-start
  74.5 2.3 copy.141
  76.8 2.3 copy.148
  80.3 2.3 copy.130
  82.7 2.3 copy.138
  85.0 2.3 copy.145
  87.3 5.6 convert_bitcast_fusion.1
  92.9 9.5 copy.146
  102.3 7.1 copy.177
  109.5 4.4 convert_bitcast_fusion
  113.8 9.5 copy.149
  123.3 7.1 copy.178
  130.4 4.4 convert_bitcast_fusion.3
  134.8 9.7 copy.139
  144.5 7.0 copy.175
  151.5 4.4 convert_bitcast_fusion.2
  155.9 9.5 copy.142
  165.3 6.9 copy.176
  172.3 4.4 convert_bitcast_fusion.4
  176.7 9.5 copy.135
  186.1 7.1 copy.174
  193.2 4.4 convert_bitcast_fusion.5
  197.6 9.9 copy.131
  207.5 7.2 copy.173
  214.7 12.1 %fusion.179 = f32[1536,1536]{1,0:T(8,128)} fusion(bf16[1536,1536]{1,0:T(8,128)(2,1)S(1)} %bitcast.283, bf16[1536,1536]{1,0:T(8,128)(2,1)} %bitcast.284), kind=kOutput, calls=%fused_computation.357 | convolution fusion | flops 7247757312 | bytes 18874368 | tf_op jit(solution)/shard_map/dot_general | solution.py:59
  226.8 10.0 fusion.178
  236.8 14.9 %add_add_fusion = f32[1536,1536]{1,0:T(8,128)} fusion(f32[1536,1536]{1,0:T(8,128)} %fusion.178, f32[1536,1536]{1,0:T(8,128)} %fusion.179, bf16[1536,1536]{1,0:T(8,128)(2,1)S(1)} %bitcast.277, bf16[1536,1536]{1,0:T(8,128)(2,1)S(1)} %bitcast.280), kind=kOutput, calls=%fused_computation.270 | convolution fusion | flops 7252475904 | bytes 37748736 | tf_op jit(solution)/shard_map/dot_general | solution.py:59
  251.8 8.5 conditional.2
  251.8 4.9 broadcast.587.clone
  260.3 4.8 broadcast_select_fusion
  265.1 567.9 %all-reduce.3.cloned.1.call-done = f32[1536,1536]{1,0:T(8,128)} async-done(((f32[1536,1536]{1,0:T(8,128)}), f32[1536,1536]{1,0:T(8,128)}) %all-reduce.3.cloned.1.call-update) | async-done | bytes 9437200 | tf_op jit(solution)/shard_map/psum | solution.py:11
  833.0 240.3 %conditional.3 = (f32[1536,1536]{1,0:T(8,128)}) conditional(s32[]{:T(128)} %convert_element_type.72, (f32[1536,1536]{1,0:T(8,128)}, f32[1536,1536]{1,0:T(8,128)}) %tuple.22, f32[1536,1536]{1,0:T(8,128)} %all-reduce.3.cloned.1.call-done), branch_computations={%region_34.35_spmd, %region_35.36_spmd} | conditional | flops 23566024704 | bytes 206569920 | solution.py:106
  833.0 8.4 fusion
  841.4 35.4 %while.1 = (s32[]{:T(128)}, f32[1536,1536]{1,0:T(8,128)}, s32[12,2]{0,1:T(2,128)S(1)}, f32[12,128,128]{2,1,0:T(8,128)S(1)}, s32[]{:T(128)}) while((s32[]{:T(128)}, f32[1536,1536]{1,0:T(8,128)}, s32[12,2]{0,1:T(2,128)S(1)}, f32[12,128,128]{2,1,0:T(8,128)S(1)}, s32[]{:T(128)}) %tuple.136), condition=%wide.while_cond, body=%wide.while_body.sunk | while | flops 2 | bytes 131189 | solution.py:107
  842.1 2.3 bitcast_dynamic-update-slice_fusion.2
  845.0 2.3 bitcast_dynamic-update-slice_fusion.2
  848.0 2.3 bitcast_dynamic-update-slice_fusion.2
  850.9 2.3 bitcast_dynamic-update-slice_fusion.2
  853.9 2.3 bitcast_dynamic-update-slice_fusion.2
  856.9 2.3 bitcast_dynamic-update-slice_fusion.2
  859.8 2.3 bitcast_dynamic-update-slice_fusion.2
  862.8 2.3 bitcast_dynamic-update-slice_fusion.2
  876.9 118.3 %custom-call.117 = f32[12,128,128]{1,2,0:T(8,128)S(1)} custom-call(f32[12,128,128]{2,1,0:T(8,128)S(1)} %get-tuple-element.38), custom_call_target="InvertDiagBlocksLowerTriangular" | custom-call | tf_op jit(solution)/shard_map/cond/branch_0_fun/jit(_solve_triangular)/triangular_solve | solution.py:107
  995.2 3.9 constant_dynamic-update-slice_fusion.55
  1001.0 2.7 constant_dynamic-update-slice_fusion.54
  1005.6 2.6 constant_dynamic-update-slice_fusion.53
  1008.2 2.5 convolution_subtract_fusion.6
  1010.7 2.9 constant_dynamic-update-slice_fusion.52
  1015.9 3.0 fusion.9
  1018.9 2.8 constant_dynamic-update-slice_fusion.51
  1021.7 4.8 convolution_subtract_fusion.5
  1026.6 2.5 constant_dynamic-update-slice_fusion.50
  1029.1 5.1 convolution_subtract_fusion.9
  1036.5 4.3 convolution_subtract_fusion.4
  1043.0 6.0 convolution_subtract_fusion
  1050.8 5.2 convolution_subtract_fusion.1
  1057.8 5.4 convolution_subtract_fusion.3
  1064.9 6.3 convolution_subtract_fusion.8
  (142 shorter events, 57.5 us)
Async XLA Ops:
  6.5 30.4 %copy-start.7 = (bf16[72,512]{1,0:T(8,128)(2,1)S(1)}, bf16[72,512]{1,0:T(8,128)(2,1)}, u32[]{:S(2)}) copy-start(bf16[72,512]{1,0:T(8,128)(2,1)} %param.9) | copy-start | bytes 221188
  13.5 33.1 %all-to-all-start.1 = ((s32[4,128,12]{2,0,1:T(4,128)}), s32[4,128,12]{2,0,1:T(4,128)S(1)}, u32[]{:S(2)}, u32[]{:S(2)}) async-start(s32[4,128,12]{2,0,1:T(4,128)} %copy.127), calls=%async_computation.1 | async-start | bytes 524288 | tf_op jit(solution)/shard_map/all_to_all | solution.py:86
  46.6 15.1 %all-to-all-start.2 = ((bf16[128,2,432]{2,1,0:T(2,128)(2,1)}), bf16[128,2,432]{2,1,0:T(2,128)(2,1)S(1)}, u32[]{:S(2)}, u32[]{:S(2)}) async-start(bf16[128,2,432]{2,1,0:T(2,128)(2,1)} %reshape.382), calls=%async_computation.2 | async-start | bytes 524288 | tf_op jit(solution)/shard_map/all_to_all | solution.py:85
  61.6 17.5 %all-to-all-start = ((bf16[128,2,432]{2,1,0:T(2,128)(2,1)}), bf16[128,2,432]{2,1,0:T(2,128)(2,1)S(1)}, u32[]{:S(2)}, u32[]{:S(2)}) async-start(bf16[128,2,432]{2,1,0:T(2,128)(2,1)} %reshape.380), calls=%async_computation | async-start | bytes 524288 | tf_op jit(solution)/shard_map/all_to_all | solution.py:84
  71.9 761.1 %all-reduce.3.cloned.1.call-start = ((), (), s32[]{:S(2)}) async-start(), calls=%async_computation.3 | async-start | bytes 18874368 | tf_op jit(solution)/shard_map/psum | solution.py:11
  102.3 7.1 copy-start.4
  123.3 7.1 copy-start.6
  144.5 7.0 copy-start.3
  186.1 7.1 copy-start.5
  207.5 7.2 slice-start.7
  207.5 7.2 slice-start.8
  207.5 19.3 %slice-start.9 = ((s8[4718592]{0:T(1024)(128)(4,1)}), s8[4194304]{0:T(1024)(128)(4,1)S(1)}, s32[]{:S(2)}) async-start(s8[4718592]{0:T(1024)(128)(4,1)} %bitcast.285), calls=%async_computation.13 | async-start | bytes 8388608
  214.7 12.1 %slice-start.10 = ((s8[4718592]{0:T(1024)(128)(4,1)}), s8[524288]{0:T(1024)(128)(4,1)S(1)}, s32[]{:S(2)}) async-start(s8[4718592]{0:T(1024)(128)(4,1)} %bitcast.285), calls=%async_computation.14 | async-start | bytes 1048576
  214.7 12.1 %copy-start.2 = (bf16[192,8,3,512]{3,1,2,0:T(8,128)(2,1)S(1)}, bf16[192,8,3,512]{3,1,2,0:T(8,128)(2,1)}, u32[]{:S(2)}) copy-start(bf16[192,8,3,512]{3,1,2,0:T(8,128)(2,1)} %copy.173) | copy-start | bytes 14155780
  214.7 22.1 %slice-start.3 = ((s8[4718592]{0:T(1024)(128)(4,1)}), s8[4194304]{0:T(1024)(128)(4,1)S(1)}, s32[]{:S(2)}) async-start(s8[4718592]{0:T(1024)(128)(4,1)} %bitcast.275), calls=%async_computation.7 | async-start | bytes 8388608
  214.7 22.1 %slice-start.5 = ((s8[4718592]{0:T(1024)(128)(4,1)}), s8[4194304]{0:T(1024)(128)(4,1)S(1)}, s32[]{:S(2)}) async-start(s8[4718592]{0:T(1024)(128)(4,1)} %bitcast.278), calls=%async_computation.9 | async-start | bytes 8388608
  226.8 10.0 slice-start.4
  226.8 10.0 slice-start.6
  995.1 8.5 slice-start
  995.2 8.5 slice-start.1
  1001.0 2.7 slice-start.2
  1013.7 2.2 copy-start.1
Sparse Core Ops, SparseCore 0:
  265.2 567.7 all-reduce.2
where the time goes:
time: 1090 us; the launch traced here: 1080 us
  waiting for transfers between devices  573 us (53%)
  local copies, waits for them, and re-layouts  177 us (16%)
  matrix products  145 us (13%)
  other arithmetic  137 us (13%)
  starting transfers between devices  30.1 us (3%)
  between operations  15 us (1%)
    psum x1, waiting for transfers between devices, spread(): return lax.psum(jnp.where(mine, shard, jnp.zeros_like(shard)), axis)  568 us
    another operation x3, other arithmetic, per_device(): jax.scipy.linalg.solve_triangular(lower, tile, lower=True)  127 us
    another operation x23, matrix products, per_device(): jax.scipy.linalg.solve_triangular(lower, tile, lower=True)  75.5 us
    unnamed x41, local copies, waits for them, and re-layouts  47.3 us
    another operation x40, local copies, waits for them, and re-layouts  40.2 us
    dot_general x3, matrix products, assemble(): lax.dot_general(left, right, (((1,), (1,)), ((), ())), preferred_element_...  36.9 us
    convert_element_type x3, local copies, waits for them, and re-layouts, assemble(): left = left.astype(jnp.bfloat16).reshape(order, 3 * block)  29 us
    convert_element_type x3, local copies, waits for them, and re-layouts, assemble(): right = right.astype(jnp.bfloat16).reshape(order, 3 * block)  28.4 us
  transfers between devices with their start and end apart: 4, of which 2 were waited for; matrix products, arithmetic and copies ran while one was open for 3% of the time, Pallas kernels for 0%

commit v1 on v0

v1 whole, which is shorter than its diff:
```python
import functools

import jax
import jax.numpy as jnp
import numpy as np
from jax import lax
from jax.experimental import pallas as pl
from jax.experimental.pallas import tpu as pltpu
from jax.sharding import PartitionSpec as P

F32 = jnp.float32
BF16 = jnp.bfloat16
CAMS = 256
OBS = 4
ORDER = 6 * CAMS
ROOM = 12
PAIR = 2 * ROOM
FEAT = 128
CHUNK = 256
NB = 128
SUB = 16


def iota(shape, dim):
    return lax.broadcasted_iota(jnp.int32, shape, dim)


def dot_t(left, right):
    return lax.dot_general(left, right, (((1,), (1,)), ((), ())), preferred_element_type=F32)


def dot(left, right):
    return jnp.dot(left, right, preferred_element_type=F32)


def split(x):
    high = x.astype(BF16)
    return high, (x - high.astype(F32)).astype(BF16)


def pack_kernel(agents, clusters, jac_ref, hess_ref, cam_ref, tile_ref, out_ref, feat):
    devices = agents * clusters
    local = tile_ref.shape[1]
    tiles = tile_ref[...]
    hot = iota((devices, local), 0) == tiles
    tri = (iota((local, local), 0) <= iota((local, local), 1)).astype(F32).astype(BF16)
    count = dot(hot.astype(F32).astype(BF16), tri)
    rank = jnp.sum(jnp.where(hot, count, 0.0), axis=0, keepdims=True) - 1.0
    key = tiles * 16 + rank.astype(jnp.int32)
    hess = hess_ref[...]
    high = hess.astype(BF16).astype(F32)
    rest = hess - high
    mid = rest.astype(BF16).astype(F32)
    feat[...] = jnp.zeros_like(feat)
    feat[0:72, :] = jac_ref[...].astype(F32)
    feat[72:78, :] = high
    feat[80:86, :] = mid
    feat[88:94, :] = rest - mid
    feat[96:100, :] = cam_ref[...].astype(F32)
    feat[100:101, :] = jnp.ones((1, local), F32)
    feats = feat[...].astype(BF16)
    slot = iota((PAIR, local), 0)
    own = slot < ROOM
    rows = clusters * PAIR

    def agent(b, carry):
        parts = []
        for d in range(clusters):
            want = jnp.where(own, (b * clusters + d) * 16 + slot, (b * clusters + b) * 16 + slot - ROOM)
            parts.append(jnp.where(want == key, 1.0, 0.0).astype(F32))
        pick = jnp.concatenate(parts, axis=0).astype(BF16)
        out_ref[pl.ds(pl.multiple_of(b * rows, rows), rows), :] = dot_t(pick, feats).astype(BF16)
        return carry

    lax.fori_loop(0, agents, agent, 0)


def factor_inverse(block, cols, rows16):
    nb = SUB
    lane = iota((nb, NB), 1)
    sub = iota((nb, NB), 0)
    lane_all = iota((NB, NB), 1)
    for k in range(NB // nb):
        o = nb * k
        x = block[o : o + nb, :]
        for j in range(nb):
            cols[j] = jnp.broadcast_to(x[:, o + j : o + j + 1], (nb, NB))
        inside = (lane >= o) & (lane < o + nb)
        rows16[...] = jnp.where(inside, jnp.where(lane - o == sub, 1.0, 0.0).astype(F32), x)
        s = [[None] * nb for _ in range(nb)]
        for j in range(nb):
            for i in range(j, nb):
                s[i][j] = jnp.broadcast_to(cols[j, i : i + 1, :], (8, NB))
        rows = [jnp.broadcast_to(rows16[i : i + 1, :], (8, NB)) for i in range(nb)]
        for j in range(nb):
            root = lax.rsqrt(s[j][j])
            rows[j] = rows[j] * root
            low = [None] * nb
            for i in range(j + 1, nb):
                low[i] = s[i][j] * root
            for i in range(j + 1, nb):
                for q in range(j + 1, i + 1):
                    s[i][q] = s[i][q] - low[i] * low[q]
                rows[i] = rows[i] - low[i] * rows[j]
        for i in range(nb):
            rows16[i : i + 1, :] = rows[i][0:1, :]
        done = rows16[...]
        kept = jnp.where((lane_all >= o) & (lane_all < o + nb), 0.0, block[...])
        if k < NB // nb - 1:
            high, low_part = split(done)
            left_high, left_low = split(jnp.where(lane >= o + nb, done, 0.0))
            left = jnp.concatenate([left_high, left_high, left_low], axis=0)
            right = jnp.concatenate([high, low_part, high], axis=0)
            kept = kept - lax.dot_general(left, right, (((0,), (0,)), ((), ())), preferred_element_type=F32)
        block[...] = kept
        block[o : o + nb, :] = done


def slots_of(recv_ref, source_ref, before_ref, place_ref):
    total = recv_ref.shape[0]
    sources = total // PAIR
    flag = jnp.where(iota((8, FEAT), 1) == 100, 1.0, 0.0).astype(F32).astype(BF16)
    valid = dot_t(flag, recv_ref[...])
    lane = iota((8, total), 1).astype(F32)
    source = jnp.floor((lane + 0.5) * (1.0 / PAIR))
    slot = lane - source * PAIR
    home = iota((sources, total), 0).astype(F32)
    source_row = jnp.broadcast_to(source[0:1, :], (sources, total))
    source_ref[...] = jnp.where(home == source_row, 1.0, 0.0).astype(F32).astype(BF16)
    before_ref[...] = jnp.where(home < source_row, 1.0, 0.0).astype(F32).astype(BF16)
    counts = []
    for part in range(2):
        mine = (slot < ROOM) if part == 0 else (slot >= ROOM)
        here = jnp.where(mine, valid, 0.0)
        per_source = dot_t(here.astype(BF16), source_ref[...])
        offset = dot(per_source.astype(BF16), before_ref[...])
        place = jnp.where(here > 0.5, offset + slot - part * ROOM, -1.0)
        place_ref[part : part + 1, :] = place[0:1, :].astype(jnp.int32)
        counts.append(jnp.sum(here[0:1, :]).astype(jnp.int32))
    return counts


def assemble(diagonal, part, count, recv_ref, place_ref, order_ref, spread_ref, left, right, target):
    target[...] = jnp.zeros_like(target)
    total = recv_ref.shape[0]
    left_obs = range(OBS) if diagonal else (0, 1)
    right_obs = range(OBS) if diagonal else (2, 3)

    def chunk(at, carry):
        want = iota((CHUNK, total), 0) + at * CHUNK
        pick = jnp.where(want == place_ref[part : part + 1, :], 1.0, 0.0).astype(F32).astype(BF16)
        tracks = dot(pick, recv_ref[...]).astype(BF16)
        x = dot_t(order_ref[...], tracks)
        h = x[72:80, :] + x[80:88, :] + x[88:96, :]
        a, b, c, d, e, f = (h[q : q + 1, :] for q in range(6))
        c00 = b * c - f * f
        c11 = a * c - e * e
        c22 = a * b - d * d
        c01 = e * f - d * c
        c02 = d * f - e * b
        c12 = d * e - a * f
        det = a * c00 + d * c01 + e * c02
        det = jnp.where(x[100:101, :] > 0.5, det, 1.0)
        inv = [[c00 / det, c01 / det, c02 / det], [c01 / det, c11 / det, c12 / det], [c02 / det, c12 / det, c22 / det]]
        jac = [x[24 * i : 24 * i + 24, :] for i in range(3)]
        wide_j, wide_w = [], []
        for j in range(3):
            w = jac[0] * inv[0][j] + jac[1] * inv[1][j] + jac[2] * inv[2][j]
            wide_w.append(dot(spread_ref[...], w.astype(BF16)).astype(BF16))
            wide_j.append(dot(spread_ref[...], jac[j].astype(BF16)).astype(BF16))
        cams = [jnp.broadcast_to(x[96 + o : 97 + o, :].astype(BF16), (48, CHUNK)) for o in range(OBS)]
        local_cam = jnp.floor((iota((48, CHUNK), 0).astype(F32) + 0.5) * (1.0 / 6.0))

        def rows(q, carry):
            cam = (local_cam + (8 * q).astype(F32)).astype(BF16)
            at_row = pl.ds(pl.multiple_of(q * 48, 48), 48)
            hits = [cam == cams[o] for o in range(OBS)]
            for j in range(3):
                at_col = slice(CHUNK * j, CHUNK * (j + 1))
                for obs, wide, out in ((left_obs, wide_w[j], left), (right_obs, wide_j[j], right)):
                    value = jnp.zeros((48, CHUNK), BF16)
                    for o in obs:
                        value = jnp.where(hits[o], wide[48 * o : 48 * o + 48, :], value)
                    out[at_row, at_col] = value
            return carry

        lax.fori_loop(0, ORDER // 48, rows, 0)
        step = 256
        for m in range(ORDER // step):
            at_row = slice(step * m, step * (m + 1))
            if diagonal:
                upto = slice(0, step * (m + 1))
                both = dot_t(left[at_row, :], right[upto, :]) + dot_t(right[at_row, :], left[upto, :])
                target[at_row, upto] += 0.5 * both
            else:
                target[at_row, :] += dot_t(left[at_row, :], right[...])
        return carry

    lax.fori_loop(0, (count + CHUNK - 1) // CHUNK, chunk, 0)


def solve_kernel(
    place_at, recv_ref, order_ref, spread_ref, out_ref,
    system, left, right, source, before, place, block, cols, rows16, low1, low2, wide,
):
    b, d, damp = place_at[0], place_at[1], place_at[2]
    on_diag = b == d
    own_count, diag_count = slots_of(recv_ref, source, before, place)
    own_count = jnp.where(on_diag, 0, own_count)
    assemble(False, 0, own_count, recv_ref, place, order_ref, spread_ref, left, right, out_ref)
    assemble(True, 1, diag_count, recv_ref, place, order_ref, spread_ref, left, right, system)
    scale = damp.astype(F32) / 8.0
    eye = iota((NB, NB), 0) == iota((NB, NB), 1)
    panels = ORDER // NB

    def panel(k, carry):
        here = pl.ds(pl.multiple_of(k * NB, NB), NB)
        diag = system[here, here]
        block[...] = diag
        factor_inverse(block, cols, rows16)
        inv_high, inv_low = split(block[...])
        inv_cat = jnp.concatenate([inv_high, inv_high, inv_low], axis=1)
        inv_cat2 = jnp.concatenate([inv_high, inv_low, inv_high], axis=1)
        col_high, col_low = split(system[:, here])
        col = dot_t(jnp.concatenate([col_high, col_low, col_high], axis=1), inv_cat)
        row_at = iota((ORDER, NB), 0) - k * NB
        col = jnp.where(row_at >= iota((ORDER, NB), 1), col, 0.0)
        system[:, here] = col
        low_high, low_low = split(jnp.where(row_at >= NB, col, 0.0))
        low1[...] = jnp.concatenate([low_high, low_low, low_high], axis=1)
        low2[...] = jnp.concatenate([low_high, low_high, low_low], axis=1)
        row_high, row_low = split(out_ref[here, :])
        solved = dot(inv_cat2, jnp.concatenate([row_high, row_high, row_low], axis=0))
        out_ref[here, :] = solved
        sol_high, sol_low = split(solved)
        wide[...] = jnp.concatenate([sol_high, sol_high, sol_low], axis=0)

        def trail(i, carry):
            at = pl.ds(pl.multiple_of(i * NB, NB), NB)
            rows = low1[at, :]
            out_ref[at, :] -= dot(rows, wide[...])
            system[at, :] -= dot_t(rows, low2[...])
            return carry

        lax.fori_loop(k + 1, panels, trail, 0)
        return carry

    def damped(k, carry):
        here = pl.ds(pl.multiple_of(k * NB, NB), NB)
        diag = system[here, here]
        system[here, here] = diag + jnp.where(eye, scale * (diag + 1.0), 0.0)
        return carry

    lax.fori_loop(0, panels, damped, 0)
    lax.fori_loop(0, panels, panel, 0)

    @pl.when(on_diag)
    def _():
        out_ref[...] = system[...]


def feature_order():
    order = np.zeros((FEAT, FEAT), np.float32)
    for q in range(FEAT):
        if q < 18 * OBS:
            i, rest = divmod(q, 24)
            o, r = divmod(rest, 6)
            order[q, 18 * o + 3 * r + i] = 1.0
        else:
            order[q, q] = 1.0
    return order


def feature_spread():
    wide = np.zeros((48 * OBS, 6 * OBS), np.float32)
    for row in range(48 * OBS):
        o, x = divmod(row, 48)
        wide[row, 6 * o + x % 6] = 1.0
    return wide


def solve(place_at, recv):
    total = recv.shape[0]
    vmem = pl.BlockSpec(memory_space=pltpu.VMEM)
    return pl.pallas_call(
        solve_kernel,
        out_shape=jax.ShapeDtypeStruct((ORDER, ORDER), F32),
        in_specs=[pl.BlockSpec(memory_space=pltpu.SMEM), vmem, vmem, vmem],
        out_specs=vmem,
        scratch_shapes=[
            pltpu.VMEM((ORDER, ORDER), F32),
            pltpu.VMEM((ORDER, 3 * CHUNK), BF16),
            pltpu.VMEM((ORDER, 3 * CHUNK), BF16),
            pltpu.VMEM((total // PAIR, total), BF16),
            pltpu.VMEM((total // PAIR, total), BF16),
            pltpu.VMEM((8, total), jnp.int32),
            pltpu.VMEM((NB, NB), F32),
            pltpu.VMEM((SUB, SUB, NB), F32),
            pltpu.VMEM((SUB, NB), F32),
            pltpu.VMEM((ORDER, 3 * NB), BF16),
            pltpu.VMEM((ORDER, 3 * NB), BF16),
            pltpu.VMEM((3 * NB, ORDER), BF16),
        ],
        compiler_params=pltpu.CompilerParams(vmem_limit_bytes=60 * 1024 * 1024),
        name="assemble_solve",
    )(place_at, recv, jnp.asarray(feature_order(), BF16), jnp.asarray(feature_spread(), BF16))


def pack(agents, clusters, jacobians, point_hessians, cameras, tiles):
    vmem = pl.BlockSpec(memory_space=pltpu.VMEM)
    local = tiles.shape[0]
    return pl.pallas_call(
        functools.partial(pack_kernel, agents, clusters),
        out_shape=jax.ShapeDtypeStruct((agents * clusters * PAIR, FEAT), BF16),
        in_specs=[vmem] * 4,
        out_specs=vmem,
        scratch_shapes=[pltpu.VMEM((FEAT, local), F32)],
        compiler_params=pltpu.CompilerParams(vmem_limit_bytes=32 * 1024 * 1024),
        name="pack",
    )(jacobians, point_hessians, cameras, tiles.reshape(1, local))


def per_device(jacobians, point_hessians, cameras, tiles, damping):
    agents = lax.axis_size("agent")
    clusters = lax.axis_size("cluster")
    packets = pack(agents, clusters, jacobians, point_hessians, cameras, tiles)
    packets = packets.reshape(agents * clusters, PAIR, FEAT)
    recv = lax.all_to_all(packets, ("agent", "cluster"), split_axis=0, concat_axis=0, tiled=True)
    recv = recv.reshape(agents * clusters * PAIR, FEAT)
    row = lax.axis_index("agent")
    col = lax.axis_index("cluster")
    damp = lax.dynamic_index_in_dim(damping, row, keepdims=False)
    return solve(jnp.stack([row, col, damp]).astype(jnp.int32), recv)


def solution(mesh):
    in_specs = (
        P(None, ("agent", "cluster")),
        P(None, ("agent", "cluster")),
        P(None, ("agent", "cluster")),
        P(("agent", "cluster")),
        P(),
    )
    return jax.shard_map(
        per_device, mesh=mesh, in_specs=in_specs, out_specs=P("agent", "cluster"), check_vma=False
    )
```

time: 1090 us -> 208 us (0.19)
  waiting for transfers between devices: 573 us -> 8.13 us
  Pallas kernels: 0 us -> 183 us
  local copies, waits for them, and re-layouts: 177 us -> 5.11 us
  matrix products: 145 us -> 0 us
  other arithmetic: 137 us -> 1.21 us
  starting transfers between devices: 30.1 us -> 10.1 us
  between operations: 15 us -> 0.02 us
    psum x1 -> x0, waiting for transfers between devices: 568 us -> none  [spread(): return lax.psum(jnp.where(mine, shard, jnp.zeros_like(shard)), axis)]
    pallas_call x0 -> x2, Pallas kernels: none -> 183 us  [the longest x1 179 us: solve(): pl.pallas_call(solve_kernel, out_shape=jax.ShapeDtypeStruct((ORDER, ORDER...]
    another operation x7 -> x1, other arithmetic: 127 us -> 1.21 us  [per_device(): return solve(jnp.stack([row, col, damp]).astype(jnp.int32), recv)]
    another operation x23 -> x0, matrix products: 75.5 us -> none  [per_device(): jax.scipy.linalg.solve_triangular(lower, tile, lower=True)]
    dot_general x10 -> x0, matrix products: 69.7 us -> none  [the longest x3 36.9 us: assemble(): lax.dot_general(left, right, (((1,), (1,)), ((), ())), preferred_element_...]
    convert_element_type x7 -> x0, local copies, waits for them, and re-layouts: 59.3 us -> none  [the longest x3 29 us: assemble(): left = left.astype(jnp.bfloat16).reshape(order, 3 * block)]
    unnamed x41 -> x10, local copies, waits for them, and re-layouts: 47.3 us -> 3.87 us
    another operation x41 -> x0, local copies, waits for them, and re-layouts: 40.2 us -> none
  transfers between devices with their start and end apart: 4 -> 1, of which waited for: 2 -> 1; matrix products, arithmetic and copies ran while one was open for 3% -> 1% of each run, Pallas kernels for 0% -> 0%
where the time goes in v1:
time: 208 us; the launch traced here: 207 us
  Pallas kernels  183 us (88%)
  starting transfers between devices  10.1 us (5%)
  waiting for transfers between devices  8.13 us (4%)
  local copies, waits for them, and re-layouts  5.11 us (2%)
    pallas_call x1, Pallas kernels, solve(): pl.pallas_call(solve_kernel, out_shape=jax.ShapeDtypeStruct((ORDER, ORDER...  179 us
    all_to_all x1, starting transfers between devices, per_device(): lax.all_to_all(packets, ('agent', 'cluster'), split_axis=0, concat_axis=0...  10.1 us
    all_to_all x1, waiting for transfers between devices, per_device(): lax.all_to_all(packets, ('agent', 'cluster'), split_axis=0, concat_axis=0...  8.13 us
  transfers between devices with their start and end apart: 1, of which 1 were waited for; matrix products, arithmetic and copies ran while one was open for 1% of the time, Pallas kernels for 0%

profile of v1, /device:TPU:115, one launch (start us, length us, event | category | flops | bytes accessed | tf_op | source)
XLA Modules:
  0.0 207.2 jit_solution(2704940878644164613)
XLA Ops:
  0.0 0.0 copy-start
  0.0 0.9 copy-done
  0.9 0.0 copy-start.1
  0.9 0.7 copy-done.1
  1.6 0.0 copy-start.2
  1.6 0.7 copy-done.2
  2.3 0.0 copy-start.3
  2.3 0.7 copy-done.3
  3.0 3.3 %pack.1 = bf16[3072,128]{1,0:T(8,128)(2,1)} custom-call(bf16[72,512]{1,0:T(8,128)(2,1)S(1)} %copy-done, f32[6,512]{1,0:T(8,128)S(1)} %copy-done.1, s32[4,512]{1,0:T(4,128)S(1)} %copy-done.2, s32[1,512]{1,0:T(1,128)S(1)} %bitcast.5), custom_call_target="tpu_custom_call" | custom-call | tf_op jit(solution)/shard_map/pack/pallas_call | solution.py:312
  6.3 10.1 %all-to-all-start = ((bf16[128,24,128]{2,1,0:T(8,128)(2,1)}), bf16[128,24,128]{2,1,0:T(8,128)(2,1)S(1)}, u32[]{:S(2)}, u32[]{:S(2)}) async-start(bf16[128,24,128]{2,1,0:T(8,128)(2,1)} %bitcast.3), calls=%async_computation | async-start | bytes 1572864 | tf_op jit(solution)/shard_map/all_to_all | solution.py:328
  16.3 1.2 dynamic_slice.4
  17.6 1.2 pad_add_fusion.place_at
  18.8 8.1 %all-to-all-done = bf16[128,24,128]{2,1,0:T(8,128)(2,1)S(1)} async-done(((bf16[128,24,128]{2,1,0:T(8,128)(2,1)}), bf16[128,24,128]{2,1,0:T(8,128)(2,1)S(1)}, u32[]{:S(2)}, u32[]{:S(2)}) %all-to-all-start) | async-done | bytes 786464 | tf_op jit(solution)/shard_map/all_to_all | solution.py:328
  26.9 0.0 copy-start.4
  26.9 0.9 copy-done.4
  27.8 179.4 %assemble_solve.1 = f32[1536,1536]{1,0:T(8,128)} custom-call(s32[3]{0:T(128)} %pad_add_fusion.place_at, bf16[3072,128]{1,0:T(8,128)(2,1)} %bitcast.6, bf16[128,128]{1,0:T(8,128)(2,1)} %constant.19.clone.order_ref, bf16[192,24]{1,0:T(8,128)(2,1)} %constant.20.clone.spread_ref), custom_call_target="tpu_custom_call" | custom-call | tf_op jit(solution)/shard_map/assemble_solve/pallas_call | solution.py:285
Async XLA Ops:
  0.0 0.9 copy-start
  0.9 0.7 copy-start.1
  1.6 0.7 copy-start.2
  2.3 0.7 copy-start.3
  6.3 20.7 %all-to-all-start = ((bf16[128,24,128]{2,1,0:T(8,128)(2,1)}), bf16[128,24,128]{2,1,0:T(8,128)(2,1)S(1)}, u32[]{:S(2)}, u32[]{:S(2)}) async-start(bf16[128,24,128]{2,1,0:T(8,128)(2,1)} %bitcast.3), calls=%async_computation | async-start | bytes 1572864 | tf_op jit(solution)/shard_map/all_to_all | solution.py:328
  26.9 0.9 copy-start.4

commit v2 on v1

--- a/solution.py
+++ b/solution.py
@@ -18,7 +18,10 @@
 FEAT = 128
 CHUNK = 256
 NB = 128
-SUB = 16
+INTERLEAVE = True
+SEGMENTS = (0, 3, 6, 9, 11)
+SUB = 32
+PAIRED = 2
 
 
 def iota(shape, dim):
@@ -75,45 +78,73 @@
     lax.fori_loop(0, agents, agent, 0)
 
 
-def factor_inverse(block, cols, rows16):
-    nb = SUB
+def factor_inverse(block, cols, rows):
+    nb, group = SUB, PAIRED
+    tall = nb // 8
     lane = iota((nb, NB), 1)
     sub = iota((nb, NB), 0)
     lane_all = iota((NB, NB), 1)
+
+    def spread(x, at):
+        return jnp.broadcast_to(x[at : at + 1, :], (8, NB))
+
     for k in range(NB // nb):
         o = nb * k
         x = block[o : o + nb, :]
         for j in range(nb):
             cols[j] = jnp.broadcast_to(x[:, o + j : o + j + 1], (nb, NB))
+        yield
         inside = (lane >= o) & (lane < o + nb)
-        rows16[...] = jnp.where(inside, jnp.where(lane - o == sub, 1.0, 0.0).astype(F32), x)
-        s = [[None] * nb for _ in range(nb)]
-        for j in range(nb):
-            for i in range(j, nb):
-                s[i][j] = jnp.broadcast_to(cols[j, i : i + 1, :], (8, NB))
-        rows = [jnp.broadcast_to(rows16[i : i + 1, :], (8, NB)) for i in range(nb)]
-        for j in range(nb):
-            root = lax.rsqrt(s[j][j])
-            rows[j] = rows[j] * root
-            low = [None] * nb
-            for i in range(j + 1, nb):
-                low[i] = s[i][j] * root
-            for i in range(j + 1, nb):
-                for q in range(j + 1, i + 1):
-                    s[i][q] = s[i][q] - low[i] * low[q]
-                rows[i] = rows[i] - low[i] * rows[j]
-        for i in range(nb):
-            rows16[i : i + 1, :] = rows[i][0:1, :]
-        done = rows16[...]
+        start = jnp.where(inside, jnp.where(lane - o == sub, 1.0, 0.0).astype(F32), x)
+        col = [[cols[j, 8 * h : 8 * h + 8, :] for h in range(tall)] for j in range(nb)]
+        row = [start[8 * h : 8 * h + 8, :] for h in range(tall)]
+        for j in range(0, nb, group):
+            first = j // 8
+            ends = (j + group) % 8 == 0
+            s = [[spread(col[j + c][first], (j + a) % 8) if c <= a else None for c in range(group)] for a in range(group)]
+            low = [[None] * group for _ in range(group)]
+            root = [None] * group
+            for c in range(group):
+                root[c] = lax.rsqrt(s[c][c])
+                for a in range(c + 1, group):
+                    low[a][c] = s[a][c] * root[c]
+                for a in range(c + 1, group):
+                    for e in range(c + 1, a + 1):
+                        s[a][e] = s[a][e] - low[a][c] * low[e][c]
+            under = [[None] * tall for _ in range(group)]
+            done = [None] * group
+            for c in range(group):
+                for h in range(first + ends, tall):
+                    part = col[j + c][h]
+                    for e in range(c):
+                        part = part - under[e][h] * low[c][e]
+                    under[c][h] = part * root[c]
+                part = spread(row[first], (j + c) % 8)
+                for e in range(c):
+                    part = part - done[e] * low[c][e]
+                done[c] = part * root[c]
+                rows[j + c : j + c + 1, :] = done[c][0:1, :]
+            for q in range(j + group, nb):
+                by = [spread(under[c][q // 8], q % 8) for c in range(group)]
+                for h in range(q // 8, tall):
+                    for c in range(group):
+                        col[q][h] = col[q][h] - under[c][h] * by[c]
+            for h in range(first + ends, tall):
+                for c in range(group):
+                    row[h] = row[h] - under[c][h] * done[c]
+            if ends:
+                yield
+        result = rows[...]
         kept = jnp.where((lane_all >= o) & (lane_all < o + nb), 0.0, block[...])
         if k < NB // nb - 1:
-            high, low_part = split(done)
-            left_high, left_low = split(jnp.where(lane >= o + nb, done, 0.0))
+            high, low_part = split(result)
+            left_high, left_low = split(jnp.where(lane >= o + nb, result, 0.0))
             left = jnp.concatenate([left_high, left_high, left_low], axis=0)
             right = jnp.concatenate([high, low_part, high], axis=0)
             kept = kept - lax.dot_general(left, right, (((0,), (0,)), ((), ())), preferred_element_type=F32)
         block[...] = kept
-        block[o : o + nb, :] = done
+        block[o : o + nb, :] = result
+        yield
 
 
 def slots_of(recv_ref, source_ref, before_ref, place_ref):
@@ -201,7 +232,7 @@
 
 def solve_kernel(
     place_at, recv_ref, order_ref, spread_ref, out_ref,
-    system, left, right, source, before, place, block, cols, rows16, low1, low2, wide,
+    system, left, right, source, before, place, block, cols, rows, low1, low2, wide,
 ):
     b, d, damp = place_at[0], place_at[1], place_at[2]
     on_diag = b == d
@@ -213,37 +244,91 @@
     eye = iota((NB, NB), 0) == iota((NB, NB), 1)
     panels = ORDER // NB
 
-    def panel(k, carry):
+    def work(first, k):
         here = pl.ds(pl.multiple_of(k * NB, NB), NB)
-        diag = system[here, here]
-        block[...] = diag
-        factor_inverse(block, cols, rows16)
+        base = first * NB
         inv_high, inv_low = split(block[...])
         inv_cat = jnp.concatenate([inv_high, inv_high, inv_low], axis=1)
         inv_cat2 = jnp.concatenate([inv_high, inv_low, inv_high], axis=1)
-        col_high, col_low = split(system[:, here])
-        col = dot_t(jnp.concatenate([col_high, col_low, col_high], axis=1), inv_cat)
-        row_at = iota((ORDER, NB), 0) - k * NB
-        col = jnp.where(row_at >= iota((ORDER, NB), 1), col, 0.0)
-        system[:, here] = col
-        low_high, low_low = split(jnp.where(row_at >= NB, col, 0.0))
-        low1[...] = jnp.concatenate([low_high, low_low, low_high], axis=1)
-        low2[...] = jnp.concatenate([low_high, low_high, low_low], axis=1)
-        row_high, row_low = split(out_ref[here, :])
-        solved = dot(inv_cat2, jnp.concatenate([row_high, row_high, row_low], axis=0))
-        out_ref[here, :] = solved
-        sol_high, sol_low = split(solved)
-        wide[...] = jnp.concatenate([sol_high, sol_high, sol_low], axis=0)
-
-        def trail(i, carry):
-            at = pl.ds(pl.multiple_of(i * NB, NB), NB)
-            rows = low1[at, :]
-            out_ref[at, :] -= dot(rows, wide[...])
-            system[at, :] -= dot_t(rows, low2[...])
+        tasks = []
+
+        def column():
+            rows = ORDER - base
+            col_high, col_low = split(system[base:, here])
+            col = dot_t(jnp.concatenate([col_high, col_low, col_high], axis=1), inv_cat)
+            row_at = iota((rows, NB), 0) - (k - first) * NB
+            col = jnp.where(row_at >= iota((rows, NB), 1), col, 0.0)
+            system[base:, here] = col
+            low_high, low_low = split(jnp.where(row_at >= NB, col, 0.0))
+            low1[base:, :] = jnp.concatenate([low_high, low_low, low_high], axis=1)
+            low2[base:, :] = jnp.concatenate([low_high, low_high, low_low], axis=1)
+
+        def solved(c):
+            def run():
+                row_high, row_low = split(out_ref[here, c])
+                part = dot(inv_cat2, jnp.concatenate([row_high, row_high, row_low], axis=0))
+                out_ref[here, c] = part
+                sol_high, sol_low = split(part)
+                wide[:, c] = jnp.concatenate([sol_high, sol_high, sol_low], axis=0)
+            return run
+
+        def trail_own(c):
+            def run():
+                out_ref[base + NB :, c] -= dot(low1[base + NB :, :], wide[:, c])
+            return run
+
+        def trail_system(start, stop):
+            def run():
+                system[start:, start:stop] -= dot_t(low1[start:, :], low2[start:stop, :])
+            return run
+
+        tasks.append(column)
+        step = 512
+        for c in range(0, ORDER, step):
+            tasks.append(solved(slice(c, c + step)))
+        if base + NB == ORDER:
+            return tasks
+        step = 256
+        for c in range(0, ORDER, step):
+            tasks.append(trail_own(slice(c, c + step)))
+        for c in range(base + NB, ORDER, step):
+            tasks.append(trail_system(c, min(c + step, ORDER)))
+        return tasks
+
+    def next_block(k):
+        here = pl.ds(pl.multiple_of(k * NB, NB), NB)
+        after = pl.ds(pl.multiple_of((k + 1) * NB, NB), NB)
+        inv_high, inv_low = split(block[...])
+        low_high, low_low = split(system[after, here])
+        low = dot_t(
+            jnp.concatenate([low_high, low_low, low_high], axis=1),
+            jnp.concatenate([inv_high, inv_high, inv_low], axis=1),
+        )
+        low_high, low_low = split(low)
+        gram = dot_t(
+            jnp.concatenate([low_high, low_low, low_high], axis=1),
+            jnp.concatenate([low_high, low_high, low_low], axis=1),
+        )
+        return system[after, after] - gram
+
+    def interleave(chain, tasks, steps):
+        given = 0
+        for at, _ in enumerate(chain):
+            until = min(len(tasks), (at + 1) * len(tasks) // steps + 1) if INTERLEAVE else 0
+            while given < until:
+                tasks[given]()
+                given += 1
+        for task in tasks[given:]:
+            task()
+
+    def segment(first, last):
+        def panel(k, carry):
+            tasks = work(first, k)
+            block[...] = next_block(k)
+            interleave(factor_inverse(block, cols, rows), tasks, (2 + SUB // 8) * (NB // SUB))
             return carry
 
-        lax.fori_loop(k + 1, panels, trail, 0)
-        return carry
+        lax.fori_loop(first, last, panel, 0)
 
     def damped(k, carry):
         here = pl.ds(pl.multiple_of(k * NB, NB), NB)
@@ -252,11 +337,23 @@
         return carry
 
     lax.fori_loop(0, panels, damped, 0)
-    lax.fori_loop(0, panels, panel, 0)
+    block[...] = system[0:NB, 0:NB]
+    for _ in factor_inverse(block, cols, rows):
+        pass
+    for first, last in zip(SEGMENTS[:-1], SEGMENTS[1:]):
+        segment(first, last)
+    for task in work(panels - 1, panels - 1):
+        task()
 
     @pl.when(on_diag)
     def _():
-        out_ref[...] = system[...]
+        def lower(k, carry):
+            at = pl.ds(pl.multiple_of(k * NB, NB), NB)
+            keep = iota((NB, ORDER), 0) + k * NB >= iota((NB, ORDER), 1)
+            out_ref[at, :] = jnp.where(keep, system[at, :], 0.0)
+            return carry
+
+        lax.fori_loop(0, panels, lower, 0)
 
 
 def feature_order():

time: 208 us -> 150 us (0.72)
  the two profiles are of different devices: /device:TPU:115 before, /device:TPU:77 now
where the time goes in v2:
time: 150 us
  Pallas kernels  124 us (83%)
  starting transfers between devices  10.3 us (7%)
  waiting for transfers between devices  9.03 us (6%)
  local copies, waits for them, and re-layouts  5.11 us (3%)
    pallas_call x1, Pallas kernels, solve(): pl.pallas_call(solve_kernel, out_shape=jax.ShapeDtypeStruct((ORDER, ORDER...  121 us
    all_to_all x1, starting transfers between devices, per_device(): lax.all_to_all(packets, ('agent', 'cluster'), split_axis=0, concat_axis=0...  10.3 us
    all_to_all x1, waiting for transfers between devices, per_device(): lax.all_to_all(packets, ('agent', 'cluster'), split_axis=0, concat_axis=0...  9.03 us
    unnamed x10, local copies, waits for them, and re-layouts  3.87 us
    pallas_call x1, Pallas kernels, pack(): pl.pallas_call(functools.partial(pack_kernel, agents, clusters), out_shap...  3.27 us
  transfers between devices with their start and end apart: 1, of which 1 were waited for; matrix products, arithmetic and copies ran while one was open for 2% of the time, Pallas kernels for 0%

profile of v2, /device:TPU:77, one launch (start us, length us, event | category | flops | bytes accessed | tf_op | source)
XLA Modules:
  0.0 149.9 jit_solution(545880218329919382)
XLA Ops:
  0.0 0.0 copy-start
  0.0 0.9 copy-done
  0.9 0.0 copy-start.1
  0.9 0.7 copy-done.1
  1.6 0.0 copy-start.2
  1.6 0.7 copy-done.2
  2.3 0.0 copy-start.3
  2.3 0.7 copy-done.3
  3.0 3.3 %pack.1 = bf16[3072,128]{1,0:T(8,128)(2,1)} custom-call(bf16[72,512]{1,0:T(8,128)(2,1)S(1)} %copy-done, f32[6,512]{1,0:T(8,128)S(1)} %copy-done.1, s32[4,512]{1,0:T(4,128)S(1)} %copy-done.2, s32[1,512]{1,0:T(1,128)S(1)} %bitcast.5), custom_call_target="tpu_custom_call" | custom-call | tf_op jit(solution)/shard_map/pack/pallas_call | solution.py:409
  6.3 10.3 %all-to-all-start = ((bf16[128,24,128]{2,1,0:T(8,128)(2,1)}), bf16[128,24,128]{2,1,0:T(8,128)(2,1)S(1)}, u32[]{:S(2)}, u32[]{:S(2)}) async-start(bf16[128,24,128]{2,1,0:T(8,128)(2,1)} %bitcast.3), calls=%async_computation | async-start | bytes 1572864 | tf_op jit(solution)/shard_map/all_to_all | solution.py:425
  16.6 1.2 dynamic_slice.4
  17.8 1.2 pad_add_fusion.place_at
  19.0 9.0 %all-to-all-done = bf16[128,24,128]{2,1,0:T(8,128)(2,1)S(1)} async-done(((bf16[128,24,128]{2,1,0:T(8,128)(2,1)}), bf16[128,24,128]{2,1,0:T(8,128)(2,1)S(1)}, u32[]{:S(2)}, u32[]{:S(2)}) %all-to-all-start) | async-done | bytes 786464 | tf_op jit(solution)/shard_map/all_to_all | solution.py:425
  28.0 0.0 copy-start.4
  28.0 0.9 copy-done.4
  28.9 120.9 %assemble_solve.1 = f32[1536,1536]{1,0:T(8,128)} custom-call(s32[3]{0:T(128)} %pad_add_fusion.place_at, bf16[3072,128]{1,0:T(8,128)(2,1)} %bitcast.6, bf16[128,128]{1,0:T(8,128)(2,1)} %constant.19.clone.order_ref, bf16[192,24]{1,0:T(8,128)(2,1)} %constant.20.clone.spread_ref), custom_call_target="tpu_custom_call" | custom-call | tf_op jit(solution)/shard_map/assemble_solve/pallas_call | solution.py:382
Async XLA Ops:
  0.0 0.9 copy-start
  0.9 0.7 copy-start.1
  1.6 0.7 copy-start.2
  2.3 0.7 copy-start.3
  6.3 21.8 %all-to-all-start = ((bf16[128,24,128]{2,1,0:T(8,128)(2,1)}), bf16[128,24,128]{2,1,0:T(8,128)(2,1)S(1)}, u32[]{:S(2)}, u32[]{:S(2)}) async-start(bf16[128,24,128]{2,1,0:T(8,128)(2,1)} %bitcast.3), calls=%async_computation | async-start | bytes 1572864 | tf_op jit(solution)/shard_map/all_to_all | solution.py:425
  28.0 0.9 copy-start.4
